TPU v7x, 32 devices: a whole 2x2x4 slice. The times are simulated.
32 devices in a mesh: lat: 8 (over y, x, core), lon: 4 (over z).
Axes of the slice: x: 2, y: 2, z: 4, core: 2. Of those that a mesh axis runs over, the one named last changes fastest.
Arguments:
- tracers: float32 [3, 1, 128, 1536], P(None, None, 'lat', 'lon'), may hold values from -6 to 6
- lon_offsets: int32 [128], P('lat'), may hold values from -190 to 190, as said below
- lon_weights: float32 [4, 128], P(None, 'lat'), may hold values from -0.25 to 0.75
- lat_offsets: int32 [128], replicated, may hold values from -4 to 4, as said below
- lat_weights: float32 [4, 128], replicated, may hold values from -0.25 to 0.75
Outputs:
- advected: float32 [3, 1, 128, 1536], P(None, None, 'lat', 'lon')
Inputs may be any that keep to these rules, and one draw needn't show every extreme that they name: `lon_offsets`: magnitudes are larger in the polar quarters of the rows; the bound is reached in every draw. `lat_offsets`: the bound is reached in every draw.
All inputs are finite; a program needn't handle non-finite values.
Results may differ from a plain program's by a relative error of at most 0.0003.
Values sent between devices are 32-bit elements; how exact they have to be, the bound alone decides.
A program may use at most 64 MiB of HBM per device.

v0:
```python
import jax
import jax.numpy as jnp
from jax import lax
from jax.sharding import PartitionSpec as P


def padded_2(block, sides, width, periodic):
    for axis, dim in sides:
        count = lax.axis_size(axis)
        forward = [(i, i + 1) for i in range(count - 1)]
        if periodic:
            forward.append((count - 1, 0))
        backward = [(target, source) for source, target in forward]
        low = lax.ppermute(
            lax.slice_in_dim(block, block.shape[dim] - width, None, axis=dim), axis, forward
        )
        high = lax.ppermute(lax.slice_in_dim(block, 0, width, axis=dim), axis, backward)
        block = jnp.concatenate([low, block, high], axis=dim)
    return block


def row_taps(row, shift, taps, base, length):
    total = jnp.zeros(row.shape[:-1] + (length,), jnp.float32)
    for k in range(4):
        start = base - shift - 1 + k
        total = total + taps[k] * lax.dynamic_slice_in_dim(row, start, length, axis=row.ndim - 1)
    return total


def per_device(tracers, lon_offsets, lon_weights, lat_offsets, lat_weights):
    rows = tracers.shape[2]
    width = tracers.shape[3]
    reach = width // 2
    nlat = lat_offsets.shape[0]
    padded = padded_2(tracers, (("lon", 3),), reach, True)
    swept = jax.vmap(
        lambda r, s, w: row_taps(r, s, w, reach, width), in_axes=(2, 0, 1), out_axes=2
    )(padded, lon_offsets, lon_weights)
    depth = rows // 4 + 2
    extended = padded_2(swept, (("lat", 2),), depth, False)
    start = lax.axis_index("lat") * rows
    own_offsets = lax.dynamic_slice_in_dim(lat_offsets, start, rows)
    own_weights = lax.dynamic_slice_in_dim(lat_weights, start, rows, axis=1)
    global_rows = start + jnp.arange(rows, dtype=jnp.int32)
    total = jnp.zeros(swept.shape, jnp.float32)
    for k in range(4):
        source = jnp.clip(global_rows - own_offsets - 1 + k, 0, nlat - 1) - start + depth
        total = total + own_weights[k][:, None] * jnp.take(extended, source, axis=2)
    return total


def solution(mesh):
    return jax.shard_map(
        per_device,
        mesh=mesh,
        in_specs=(P(None, None, "lat", "lon"), P("lat"), P(None, "lat"), P(), P()),
        out_specs=P(None, None, "lat", "lon"),
        check_vma=False,
    )
```

profile of v0, /device:TPU:1, one launch (start us, length us, event | category | flops | bytes accessed | tf_op | source)
XLA Modules:
  0.0 77.3 jit_solution(11217653338937780925)
XLA Ops:
  0.0 0.0 copy-start
  0.0 0.9 %fusion.20 = (f32[3,1,16,192]{3,2,1,0:T(8,128)S(1)}, f32[3,1,16,192]{3,2,1,0:T(8,128)S(1)}) fusion(f32[3,1,16,384]{3,2,1,0:T(8,128)} %param.7), kind=kLoop, calls=%fused_computation.69 | loop fusion | bytes 147456 | tf_op jit(solution)/shard_map/slice | solution.py:15
  1.0 2.1 %collective-permute-start = (f32[3,1,16,192]{3,2,1,0:T(8,128)S(1)}, f32[3,1,16,192]{3,2,1,0:T(8,128)S(1)}, u32[]{:S(2)}, u32[]{:S(2)}) collective-permute-start(f32[3,1,16,192]{3,2,1,0:T(8,128)S(1)} %get-tuple-element.16), channel_id=1, source_target_pairs={{0,1},{1,2},{2,3},{3,0},{4,5},{5,6},{6,7},{7,4},{8,9},{9,10},{10,1... | collective-permute-start | bytes 110600 | tf_op jit(solution)/shard_map/ppermute | solution.py:14
  3.1 2.1 %collective-permute-start.1 = (f32[3,1,16,192]{3,2,1,0:T(8,128)S(1)}, f32[3,1,16,192]{3,2,1,0:T(8,128)S(1)}, u32[]{:S(2)}, u32[]{:S(2)}) collective-permute-start(f32[3,1,16,192]{3,2,1,0:T(8,128)S(1)} %get-tuple-element.17), channel_id=1, source_target_pairs={{1,0},{2,1},{3,2},{0,3},{5,4},{6,5},{7,6},{4,7},{9,8},{10,9},{11,1... | collective-permute-start | bytes 110600 | tf_op jit(solution)/shard_map/ppermute | solution.py:17
  5.2 0.7 fusion.18
  5.8 0.8 %slice_bitcast_fusion.6 = (f32[16]{0:T(128)S(1)}, f32[16]{0:T(128)S(1)}, f32[16]{0:T(128)S(1)}, f32[16]{0:T(128)S(1)}) fusion(f32[4,16]{1,0:T(4,128)} %param.9), kind=kLoop, calls=%fused_computation.65 | loop fusion | bytes 512 | tf_op jit(solution)/shard_map/vmap()/mul | solution.py:26
  6.7 0.7 compare_and_fusion.3
  7.4 0.0 copy-done
  7.4 0.1 constant_dynamic-slice_fusion
  7.5 0.0 collective-permute-done
  7.5 0.0 collective-permute-done.1
  7.5 1.0 %pad_maximum_fusion = f32[3,1,16,768]{3,2,1,0:T(8,128)S(1)} fusion(f32[3,1,16,192]{3,2,1,0:T(8,128)S(1)} %collective-permute-done.1, f32[3,1,16,384]{3,2,1,0:T(8,128)} %param.7, f32[3,1,16,192]{3,2,1,0:T(8,128)S(1)} %collective-permute-done), kind=kLoop, calls=%fused_computation.17 | loop fusion | flops 73728 | bytes 294912 | tf_op jit(solution)/shard_map/concatenate | solution.py:18
  8.5 6.6 %copy.37 = f32[3,1,16,768]{0,1,2,3:T(1,128)} copy(f32[3,1,16,768]{3,2,1,0:T(8,128)S(1)} %pad_maximum_fusion) | data formatting | bytes 294912 | tf_op jit(solution)/shard_map/concatenate | solution.py:18
  15.1 6.5 %gather_fusion = f32[16,3,384]{1,0,2:T(8,128)} fusion(f32[16,3,1,768]{1,2,0,3:T(1,128)} %bitcast.103, s32[16]{0:T(128)S(1)} %get-tuple-element.32), kind=kCustom, calls=%fused_computation.4 | custom fusion | bytes 147712 | tf_op jit(solution)/shard_map/vmap()/gather | solution.py:26
  21.7 6.5 %gather_fusion.1 = f32[16,3,384]{1,0,2:T(8,128)} fusion(f32[16,3,1,768]{1,2,0,3:T(1,128)} %bitcast.104, s32[16]{0:T(128)S(1)} %get-tuple-element.33), kind=kCustom, calls=%fused_computation.5 | custom fusion | bytes 147712 | tf_op jit(solution)/shard_map/vmap()/gather | solution.py:26
  28.2 6.5 %gather_fusion.2 = f32[16,3,384]{1,0,2:T(8,128)} fusion(f32[16,3,1,768]{1,2,0,3:T(1,128)} %bitcast.105, s32[16]{0:T(128)S(1)} %get-tuple-element.35), kind=kCustom, calls=%fused_computation.6 | custom fusion | bytes 147712 | tf_op jit(solution)/shard_map/vmap()/gather | solution.py:26
  34.7 6.6 %gather_fusion.3 = f32[16,3,384]{1,0,2:T(8,128)} fusion(f32[16,3,1,768]{1,2,0,3:T(1,128)} %bitcast.106, s32[16]{0:T(128)S(1)} %get-tuple-element.34), kind=kCustom, calls=%fused_computation.7 | custom fusion | bytes 147712 | tf_op jit(solution)/shard_map/vmap()/gather | solution.py:26
  41.3 5.5 %fusion.1 = f32[3,1,16,384]{0,2,3,1:T(8,128)S(1)} fusion(f32[16,3,384]{1,0,2:T(8,128)} %gather_fusion.3, f32[16,3,384]{1,0,2:T(8,128)} %gather_fusion.2, f32[16,3,384]{1,0,2:T(8,128)} %gather_fusion.1, f32[16,3,384]{1,0,2:T(8,128)} %gather_fusion, f32[16]{0:T(128)S(1)} %get-tuple-element.24, f32[16]{0:T(128)S(1)} %get-tuple-element.25, ...), kind=kLoop, calls=%fused_computation.11 | loop fusion | flops 129024 | bytes 368896 | tf_op jit(solution)/shard_map/vmap()/transpose | solution.py:36
  46.8 1.9 %fusion.19 = (f32[3,1,6,384]{0,2,3,1:T(8,128)}, f32[3,1,6,384]{0,2,3,1:T(8,128)}) fusion(f32[3,1,16,384]{0,2,3,1:T(8,128)S(1)} %fusion.1), kind=kLoop, calls=%fused_computation.68 | loop fusion | bytes 110592 | tf_op jit(solution)/shard_map/slice | solution.py:15
  48.7 1.8 %copy.38 = f32[3,1,6,384]{3,1,2,0:T(1,128)S(1)} copy(f32[3,1,6,384]{0,2,3,1:T(8,128)} %get-tuple-element.14) | data formatting | bytes 55296 | tf_op jit(solution)/shard_map/slice | solution.py:15
  50.5 4.1 %collective-permute-start.2 = (f32[3,1,6,384]{3,1,2,0:T(1,128)S(1)}, f32[3,1,6,384]{3,1,2,0:T(1,128)S(1)}, u32[]{:S(2)}, u32[]{:S(2)}) collective-permute-start(f32[3,1,6,384]{3,1,2,0:T(1,128)S(1)} %copy.38), channel_id=1, source_target_pairs={{0,4},{4,8},{8,12},{12,16},{16,20},{20,24},{24,28},{1,5},{5,9},{9,... | collective-permute-start | bytes 82952 | tf_op jit(solution)/shard_map/ppermute | solution.py:14
  54.6 1.8 %copy.39 = f32[3,1,6,384]{3,1,2,0:T(1,128)S(1)} copy(f32[3,1,6,384]{0,2,3,1:T(8,128)} %get-tuple-element.15) | data formatting | bytes 55296 | tf_op jit(solution)/shard_map/slice | solution.py:17
  56.4 2.1 %collective-permute-start.3 = (f32[3,1,6,384]{3,1,2,0:T(1,128)S(1)}, f32[3,1,6,384]{3,1,2,0:T(1,128)S(1)}, u32[]{:S(2)}, u32[]{:S(2)}) collective-permute-start(f32[3,1,6,384]{3,1,2,0:T(1,128)S(1)} %copy.39), channel_id=1, source_target_pairs={{4,0},{8,4},{12,8},{16,12},{20,16},{24,20},{28,24},{5,1},{9,5},{13... | collective-permute-start | bytes 82952 | tf_op jit(solution)/shard_map/ppermute | solution.py:17
  58.5 0.0 collective-permute-done.2
  58.5 1.8 %copy.40 = f32[3,1,6,384]{0,2,3,1:T(8,128)} copy(f32[3,1,6,384]{3,1,2,0:T(1,128)S(1)} %collective-permute-done.2) | data formatting | bytes 55296 | tf_op jit(solution)/shard_map/ppermute | solution.py:14
  60.3 1.3 %collective-permute-done.3 = f32[3,1,6,384]{3,1,2,0:T(1,128)S(1)} collective-permute-done((f32[3,1,6,384]{3,1,2,0:T(1,128)S(1)}, f32[3,1,6,384]{3,1,2,0:T(1,128)S(1)}, u32[]{:S(2)}, u32[]{:S(2)}) %collective-permute-start.3) | collective-permute-done | bytes 27680 | tf_op jit(solution)/shard_map/ppermute | solution.py:17
  61.6 1.7 %copy.41 = f32[3,1,6,384]{0,2,3,1:T(8,128)} copy(f32[3,1,6,384]{3,1,2,0:T(1,128)S(1)} %collective-permute-done.3) | data formatting | bytes 55296 | tf_op jit(solution)/shard_map/ppermute | solution.py:17
  63.2 5.8 %maximum_bitcast_fusion = f32[3,28,384]{0,1,2:T(8,128)} fusion(f32[3,1,6,384]{0,2,3,1:T(8,128)} %copy.41, f32[3,1,16,384]{0,2,3,1:T(8,128)S(1)} %fusion.1, f32[3,1,6,384]{0,2,3,1:T(8,128)} %copy.40), kind=kLoop, calls=%fused_computation.8 | loop fusion | flops 64512 | bytes 258048 | tf_op jit(solution)/shard_map/jit(_take)/Arg_0.5 | solution.py:48
  69.0 5.1 %copy.42 = f32[3,28,384]{2,0,1:T(4,128)S(1)} copy(f32[3,28,384]{0,1,2:T(8,128)} %maximum_bitcast_fusion) | data formatting | bytes 258048 | tf_op jit(solution)/shard_map/jit(_take)/Arg_0.5 | solution.py:48
  74.1 0.6 gather_fusion.6
  74.8 0.6 gather_fusion.4
  75.4 0.6 gather_fusion.5
  76.0 0.6 gather_fusion.7
  76.6 0.7 fusion.5
  (3 shorter events, 0.0 us)
Async XLA Ops:
  0.0 7.4 %copy-start = (f32[4,128]{1,0:T(4,128)S(1)}, f32[4,128]{1,0:T(4,128)}, u32[]{:S(2)}) copy-start(f32[4,128]{1,0:T(4,128)} %param.11) | copy-start | bytes 6148
  1.0 6.6 %collective-permute-start = (f32[3,1,16,192]{3,2,1,0:T(8,128)S(1)}, f32[3,1,16,192]{3,2,1,0:T(8,128)S(1)}, u32[]{:S(2)}, u32[]{:S(2)}) collective-permute-start(f32[3,1,16,192]{3,2,1,0:T(8,128)S(1)} %get-tuple-element.16), channel_id=1, source_target_pairs={{0,1},{1,2},{2,3},{3,0},{4,5},{5,6},{6,7},{7,4},{8,9},{9,10},{10,1... | collective-permute-start | bytes 110600 | tf_op jit(solution)/shard_map/ppermute | solution.py:14
  3.1 4.4 %collective-permute-start.1 = (f32[3,1,16,192]{3,2,1,0:T(8,128)S(1)}, f32[3,1,16,192]{3,2,1,0:T(8,128)S(1)}, u32[]{:S(2)}, u32[]{:S(2)}) collective-permute-start(f32[3,1,16,192]{3,2,1,0:T(8,128)S(1)} %get-tuple-element.17), channel_id=1, source_target_pairs={{1,0},{2,1},{3,2},{0,3},{5,4},{6,5},{7,6},{4,7},{9,8},{10,9},{11,1... | collective-permute-start | bytes 110600 | tf_op jit(solution)/shard_map/ppermute | solution.py:17
  50.5 8.0 %collective-permute-start.2 = (f32[3,1,6,384]{3,1,2,0:T(1,128)S(1)}, f32[3,1,6,384]{3,1,2,0:T(1,128)S(1)}, u32[]{:S(2)}, u32[]{:S(2)}) collective-permute-start(f32[3,1,6,384]{3,1,2,0:T(1,128)S(1)} %copy.38), channel_id=1, source_target_pairs={{0,4},{4,8},{8,12},{12,16},{16,20},{20,24},{24,28},{1,5},{5,9},{9,... | collective-permute-start | bytes 82952 | tf_op jit(solution)/shard_map/ppermute | solution.py:14
  56.4 5.2 %collective-permute-start.3 = (f32[3,1,6,384]{3,1,2,0:T(1,128)S(1)}, f32[3,1,6,384]{3,1,2,0:T(1,128)S(1)}, u32[]{:S(2)}, u32[]{:S(2)}) collective-permute-start(f32[3,1,6,384]{3,1,2,0:T(1,128)S(1)} %copy.39), channel_id=1, source_target_pairs={{4,0},{8,4},{12,8},{16,12},{20,16},{24,20},{28,24},{5,1},{9,5},{13... | collective-permute-start | bytes 82952 | tf_op jit(solution)/shard_map/ppermute | solution.py:17
where the time goes:
time: 77.9 us; the launch traced here: 77.3 us
  local copies, waits for them, and re-layouts  51 us (65%)
  other arithmetic  14.5 us (19%)
  starting transfers between devices  10.5 us (13%)
  waiting for transfers between devices  1.3 us (2%)
    gather x4, local copies, waits for them, and re-layouts, row_taps(): lax.dynamic_slice_in_dim(row, start, length, axis=row.ndim - 1)  26.2 us
    concatenate x1, local copies, waits for them, and re-layouts, padded_2(): block = jnp.concatenate([low, block, high], axis=dim)  6.6 us
    ppermute x2, starting transfers between devices, padded_2(): lax.ppermute(lax.slice_in_dim(block, block.shape[dim] - width, None, axis...  6.27 us
    another operation x1, other arithmetic, per_device(): total = total + own_weights[k][:, None] * jnp.take(extended, source, axis=2)  5.81 us
    transpose x1, other arithmetic, per_device(): jax.vmap(lambda r, s, w: row_taps(r, s, w, reach, width), in_axes=(2, 0,...  5.52 us
    another operation x1, local copies, waits for them, and re-layouts, per_device(): total = total + own_weights[k][:, None] * jnp.take(extended, source, axis=2)  5.1 us
    slice x3, local copies, waits for them, and re-layouts, padded_2(): lax.slice_in_dim(block, block.shape[dim] - width, None, axis=dim)  4.56 us
    ppermute x2, starting transfers between devices, padded_2(): lax.ppermute(lax.slice_in_dim(block, 0, width, axis=dim), axis, backward)  4.19 us
  transfers between devices with their start and end apart: 4, of which 1 were waited for; matrix products, arithmetic and copies ran while one was open for 8% of the time, Pallas kernels for 0%

commit v1 on v0

v1 whole, which is shorter than its diff:
```python
import functools

import jax
import jax.numpy as jnp
from jax import lax
from jax.experimental import pallas as pl
from jax.experimental.pallas import tpu as pltpu
from jax.sharding import PartitionSpec as P

MESH = pl.DeviceIdType.MESH
LANES = 128
HALF = 64
SUB = 8
BELOW = 5
ABOVE = 6


def kernel(n_lat, n_lon, nlat, tr, lono, lonw, lato, latw, out,
           own, send_r, send_l, from_l, from_r, ext,
           own_sem, s_lon, r_lon, s_lat, r_lat):
    fields, rows, width = own.shape
    tiles = width // LANES
    ilat = lax.axis_index("lat")
    ilon = lax.axis_index("lon")
    right = lax.rem(ilon + 1, n_lon)
    left = lax.rem(ilon + n_lon - 1, n_lon)
    has_lo = ilat > 0
    has_hi = ilat < n_lat - 1

    barrier = pltpu.get_barrier_semaphore()
    pl.semaphore_signal(barrier, inc=1, device_id=(ilat, right), device_id_type=MESH)
    pl.semaphore_signal(barrier, inc=1, device_id=(ilat, left), device_id_type=MESH)

    @pl.when(has_lo)
    def _():
        pl.semaphore_signal(barrier, inc=1, device_id=(ilat - 1, ilon), device_id_type=MESH)

    @pl.when(has_hi)
    def _():
        pl.semaphore_signal(barrier, inc=1, device_id=(ilat + 1, ilon), device_id_type=MESH)

    load = pltpu.make_async_copy(tr, own, own_sem)
    load.start()

    @pl.when(jnp.logical_not(has_lo))
    def _():
        ext[:, 0:SUB, :] = jnp.zeros((fields, SUB, width), jnp.float32)

    @pl.when(jnp.logical_not(has_hi))
    def _():
        ext[:, SUB + rows:, :] = jnp.zeros((fields, SUB, width), jnp.float32)

    lane8 = lax.broadcasted_iota(jnp.int32, (SUB, LANES), 1)
    upper8 = lane8 >= HALF
    load.wait()
    for f in range(fields):
        last = width - LANES
        send_r[f, 0:rows, :] = own[f, :, last:]
        a = own[f, 0:SUB, last - LANES:last]
        b = own[f, SUB:rows, last - LANES:last]
        send_r[f, rows:, :] = jnp.where(upper8, a, pltpu.roll(b, HALF, 1))
        send_l[f, 0:rows, :] = own[f, :, 0:LANES]
        a = own[f, 0:SUB, LANES:2 * LANES]
        b = own[f, SUB:rows, LANES:2 * LANES]
        send_l[f, rows:, :] = jnp.where(upper8, pltpu.roll(b, HALF, 1), a)

    pl.semaphore_wait(barrier, 2 + has_lo.astype(jnp.int32) + has_hi.astype(jnp.int32))

    lon_copies = []
    for f in range(fields):
        to_r = pltpu.make_async_remote_copy(
            src_ref=send_r.at[f], dst_ref=from_l.at[f], send_sem=s_lon.at[0, f],
            recv_sem=r_lon.at[0, f], device_id=(ilat, right), device_id_type=MESH)
        to_l = pltpu.make_async_remote_copy(
            src_ref=send_l.at[f], dst_ref=from_r.at[f], send_sem=s_lon.at[1, f],
            recv_sem=r_lon.at[1, f], device_id=(ilat, left), device_id_type=MESH)
        to_r.start()
        to_l.start()
        lon_copies.append((to_r, to_l))

    row = lax.broadcasted_iota(jnp.int32, (rows, 1), 0)
    start = ilat * rows

    def column(values, first):
        lanes = values.shape[1]
        pick = (lax.broadcasted_iota(jnp.int32, (rows, lanes), 1)
                == first + lax.broadcasted_iota(jnp.int32, (rows, lanes), 0))
        return jnp.sum(jnp.where(pick, values, 0.0), axis=1, keepdims=True)

    lon_off = column(lono[...].astype(jnp.float32), 0).astype(jnp.int32)
    lon_w = [column(lonw[k:k + 1, :], 0) for k in range(4)]
    lat_off = column(lato[...].astype(jnp.float32), start).astype(jnp.int32)
    lat_w = [column(latw[k:k + 1, :], start) for k in range(4)]

    source = [jnp.clip(start + row - lat_off - 1 + k, 0, nlat - 1) - start for k in range(4)]

    def coefficient(s):
        total = jnp.zeros((rows, 1), jnp.float32)
        for k in range(4):
            total = total + jnp.where(source[k] == s, lat_w[k], 0.0)
        return total

    coef = {s: coefficient(s) for s in range(-BELOW, rows + ABOVE)}

    first = jnp.broadcast_to(2 * LANES - 1 - lon_off, (rows, LANES))
    coarse = first >> 7
    fine = first & (LANES - 1)
    lane = lax.broadcasted_iota(jnp.int32, (rows, LANES), 1)
    index = (lane + fine) & (LANES - 1)
    inside = lane < LANES - fine
    is_q = [coarse == q for q in range(3)]

    def lat_copies(f):
        up = pltpu.make_async_remote_copy(
            src_ref=ext.at[f, pl.ds(rows, SUB)], dst_ref=ext.at[f, pl.ds(0, SUB)],
            send_sem=s_lat.at[0, f], recv_sem=r_lat.at[0, f],
            device_id=(ilat + 1, ilon), device_id_type=MESH)
        down = pltpu.make_async_remote_copy(
            src_ref=ext.at[f, pl.ds(SUB, SUB)], dst_ref=ext.at[f, pl.ds(SUB + rows, SUB)],
            send_sem=s_lat.at[1, f], recv_sem=r_lat.at[1, f],
            device_id=(ilat - 1, ilon), device_id_type=MESH)
        return up, down

    partial = []
    for f in range(fields):
        to_r, to_l = lon_copies[f]
        to_r.wait_recv()
        to_l.wait_recv()
        tail_l = from_l[f, rows:, :]
        tail_r = from_r[f, rows:, :]
        x = [jnp.concatenate([tail_l, pltpu.roll(tail_l, HALF, 1)], axis=0), from_l[f, 0:rows, :]]
        x += [own[f, :, i * LANES:(i + 1) * LANES] for i in range(tiles)]
        x += [from_r[f, 0:rows, :], jnp.concatenate([tail_r, pltpu.roll(tail_r, HALF, 1)], axis=0)]
        z = []
        for t in range(tiles + 2):
            y = x[min(t + 3, tiles + 3)]
            for q in (2, 1, 0):
                y = jnp.where(is_q[q], x[t + q], y)
            z.append(jnp.take_along_axis(y, index, axis=1, mode="promise_in_bounds"))
        b = [jnp.where(inside, z[t], z[t + 1]) for t in range(tiles + 1)]
        sums = [lon_w[0] * b[t] for t in range(tiles)]
        for k in range(1, 4):
            moved = [pltpu.roll(v, LANES - k, 1) for v in b]
            for t in range(tiles):
                sums[t] = sums[t] + lon_w[k] * jnp.where(lane < LANES - k, moved[t], moved[t + 1])
        for t in range(tiles):
            ext[f, SUB:SUB + rows, t * LANES:(t + 1) * LANES] = sums[t]
        up, down = lat_copies(f)
        pl.when(has_hi)(up.start)
        pl.when(has_lo)(down.start)

    for f in range(fields):
        low = jnp.zeros((SUB, width), jnp.float32)
        high = jnp.zeros((SUB, width), jnp.float32)
        for s in range(rows):
            line = ext[f, SUB + s:SUB + s + 1, :]
            if s < SUB + ABOVE:
                low = low + coef[s][:SUB] * line
            if s >= SUB - BELOW:
                high = high + coef[s][SUB:] * line
        partial.append((low, high))

    for f in range(fields):
        low, high = partial[f]
        up, down = lat_copies(f)
        pl.when(has_lo)(up.wait_recv)
        pl.when(has_hi)(down.wait_recv)
        for s in range(-BELOW, 0):
            low = low + coef[s][:SUB] * ext[f, SUB + s:SUB + s + 1, :]
        for s in range(rows, rows + ABOVE):
            high = high + coef[s][SUB:] * ext[f, SUB + s:SUB + s + 1, :]
        out[f, 0:SUB, :] = low
        out[f, SUB:rows, :] = high

    for f in range(fields):
        for copy in lon_copies[f]:
            copy.wait_send()
        up, down = lat_copies(f)
        pl.when(has_hi)(up.wait_send)
        pl.when(has_lo)(down.wait_send)


def per_device(n_lat, n_lon, tracers, lon_offsets, lon_weights, lat_offsets, lat_weights):
    rows, width = tracers.shape[2:]
    fields = tracers.shape[0] * tracers.shape[1]
    nlat = lat_offsets.shape[0]
    vmem = pl.BlockSpec(memory_space=pltpu.VMEM)
    out = pl.pallas_call(
        functools.partial(kernel, n_lat, n_lon, nlat),
        out_shape=jax.ShapeDtypeStruct((fields, rows, width), jnp.float32),
        in_specs=[pl.BlockSpec(memory_space=pl.ANY)] + [vmem] * 4,
        out_specs=vmem,
        scratch_shapes=[
            pltpu.VMEM((fields, rows, width), jnp.float32),
            pltpu.VMEM((fields, rows + SUB, LANES), jnp.float32),
            pltpu.VMEM((fields, rows + SUB, LANES), jnp.float32),
            pltpu.VMEM((fields, rows + SUB, LANES), jnp.float32),
            pltpu.VMEM((fields, rows + SUB, LANES), jnp.float32),
            pltpu.VMEM((fields, rows + 2 * SUB, width), jnp.float32),
            pltpu.SemaphoreType.DMA,
            pltpu.SemaphoreType.DMA((2, fields)),
            pltpu.SemaphoreType.DMA((2, fields)),
            pltpu.SemaphoreType.DMA((2, fields)),
            pltpu.SemaphoreType.DMA((2, fields)),
        ],
        compiler_params=pltpu.CompilerParams(collective_id=0, has_side_effects=True),
    )(
        tracers.reshape(fields, rows, width),
        lon_offsets.reshape(1, rows),
        lon_weights,
        lat_offsets.reshape(1, nlat),
        lat_weights,
    )
    return out.reshape(tracers.shape)


def solution(mesh):
    return jax.shard_map(
        functools.partial(per_device, mesh.shape["lat"], mesh.shape["lon"]),
        mesh=mesh,
        in_specs=(P(None, None, "lat", "lon"), P("lat"), P(None, "lat"), P(), P()),
        out_specs=P(None, None, "lat", "lon"),
        check_vma=False,
    )
```

time: 77.9 us -> 15 us (0.19)
  local copies, waits for them, and re-layouts: 51 us -> 1.52 us
  other arithmetic: 14.5 us -> 0 us
  Pallas kernels: 0 us -> 13.2 us
  starting transfers between devices: 10.5 us -> 0 us
  waiting for transfers between devices: 1.3 us -> 0 us
    gather x8 -> x0, local copies, waits for them, and re-layouts: 28.6 us -> none  [the longest x4 26.2 us: row_taps(): lax.dynamic_slice_in_dim(row, start, length, axis=row.ndim - 1)]
    pallas_call x0 -> x1, Pallas kernels: none -> 13.2 us  [per_device(): pl.pallas_call(functools.partial(kernel, n_lat, n_lon, nlat), out_shape=j...]
    ppermute x4 -> x0, starting transfers between devices: 10.5 us -> none  [the longest x2 6.27 us: padded_2(): lax.ppermute(lax.slice_in_dim(block, block.shape[dim] - width, None, axis...]
    concatenate x1 -> x0, local copies, waits for them, and re-layouts: 6.6 us -> none  [padded_2(): block = jnp.concatenate([low, block, high], axis=dim)]
    slice x4 -> x0, local copies, waits for them, and re-layouts: 6.32 us -> none  [the longest x3 4.56 us: padded_2(): lax.slice_in_dim(block, block.shape[dim] - width, None, axis=dim)]
    another operation x1 -> x0, other arithmetic: 5.81 us -> none  [per_device(): total = total + own_weights[k][:, None] * jnp.take(extended, source, axis=2)]
    transpose x1 -> x0, other arithmetic: 5.52 us -> none  [per_device(): jax.vmap(lambda r, s, w: row_taps(r, s, w, reach, width), in_axes=(2, 0,...]
    another operation x1 -> x0, local copies, waits for them, and re-layouts: 5.1 us -> none  [per_device(): total = total + own_weights[k][:, None] * jnp.take(extended, source, axis=2)]
  transfers between devices with their start and end apart: 4 -> 0, of which waited for: 1 -> 0; matrix products, arithmetic and copies ran while one was open for 8% -> 0% of each run, Pallas kernels for 0% -> 0%
where the time goes in v1:
time: 15 us; the launch traced here: 14.8 us
  Pallas kernels  13.2 us (88%)
  local copies, waits for them, and re-layouts  1.52 us (10%)
    pallas_call x1, Pallas kernels, per_device(): pl.pallas_call(functools.partial(kernel, n_lat, n_lon, nlat), out_shape=j...  13.2 us
    unnamed x1, local copies, waits for them, and re-layouts  1.52 us

profile of v1, /device:TPU:1, one launch (start us, length us, event | category | flops | bytes accessed | tf_op | source)
XLA Modules:
  0.0 14.8 jit_solution(11629344220620244214)
XLA Ops:
  0.0 13.2 %shard_map.55 = f32[3,16,384]{2,1,0:T(8,128)} custom-call(f32[3,16,384]{2,1,0:T(8,128)} %bitcast.7, s32[1,16]{1,0:T(1,128)} %bitcast.8, f32[4,16]{1,0:T(4,128)} %lonw.1, s32[1,128]{1,0:T(1,128)} %bitcast.9, f32[4,128]{1,0:T(4,128)} %latw.1), custom_call_target="tpu_custom_call" | custom-call | tf_op jit(solution)/shard_map/pallas_call | solution.py:188
  13.2 1.5 %copy.8 = f32[3,1,16,384]{3,2,1,0:T(8,128)} copy(f32[3,1,16,384]{3,2,1,0:T(8,128)} %bitcast.6) | data formatting | bytes 147456

commit v2 on v1

--- a/solution.py
+++ b/solution.py
@@ -15,9 +15,9 @@
 ABOVE = 6
 
 
-def kernel(n_lat, n_lon, nlat, tr, lono, lonw, lato, latw, out,
-           own, send_r, send_l, from_l, from_r, ext,
-           own_sem, s_lon, r_lon, s_lat, r_lat):
+def kernel(n_lat, n_lon, nlat, tr, lono_in, lonw_in, lato_in, latw_in, out,
+           own, lono, lonw, lato, latw, send_r, send_l, from_l, from_r, ext,
+           own_sem, s_par, s_lon, r_lon, s_lat, r_lat):
     fields, rows, width = own.shape
     tiles = width // LANES
     ilat = lax.axis_index("lat")
@@ -41,6 +41,13 @@
 
     load = pltpu.make_async_copy(tr, own, own_sem)
     load.start()
+    loads = [
+        pltpu.make_async_copy(source, target, s_par.at[i])
+        for i, (source, target) in enumerate(
+            ((lono_in, lono), (lonw_in, lonw), (lato_in, lato), (latw_in, latw)))
+    ]
+    for copy in loads:
+        copy.start()
 
     @pl.when(jnp.logical_not(has_lo))
     def _():
@@ -77,6 +84,9 @@
         to_r.start()
         to_l.start()
         lon_copies.append((to_r, to_l))
+
+    for copy in loads:
+        copy.wait()
 
     row = lax.broadcasted_iota(jnp.int32, (rows, 1), 0)
     start = ilat * rows
@@ -187,17 +197,22 @@
     vmem = pl.BlockSpec(memory_space=pltpu.VMEM)
     out = pl.pallas_call(
         functools.partial(kernel, n_lat, n_lon, nlat),
-        out_shape=jax.ShapeDtypeStruct((fields, rows, width), jnp.float32),
-        in_specs=[pl.BlockSpec(memory_space=pl.ANY)] + [vmem] * 4,
+        out_shape=pltpu.VMEM((fields, rows, width), jnp.float32),
+        in_specs=[pl.BlockSpec(memory_space=pl.ANY)] * 5,
         out_specs=vmem,
         scratch_shapes=[
             pltpu.VMEM((fields, rows, width), jnp.float32),
+            pltpu.VMEM((1, rows), jnp.int32),
+            pltpu.VMEM((4, rows), jnp.float32),
+            pltpu.VMEM((1, nlat), jnp.int32),
+            pltpu.VMEM((4, nlat), jnp.float32),
             pltpu.VMEM((fields, rows + SUB, LANES), jnp.float32),
             pltpu.VMEM((fields, rows + SUB, LANES), jnp.float32),
             pltpu.VMEM((fields, rows + SUB, LANES), jnp.float32),
             pltpu.VMEM((fields, rows + SUB, LANES), jnp.float32),
             pltpu.VMEM((fields, rows + 2 * SUB, width), jnp.float32),
             pltpu.SemaphoreType.DMA,
+            pltpu.SemaphoreType.DMA((4,)),
             pltpu.SemaphoreType.DMA((2, fields)),
             pltpu.SemaphoreType.DMA((2, fields)),
             pltpu.SemaphoreType.DMA((2, fields)),

time: 15 us -> 12.8 us (0.85)
  Pallas kernels: 13.2 us -> 12 us
  local copies, waits for them, and re-layouts: 1.52 us -> 0.64 us
    pallas_call x1, Pallas kernels: 13.2 us -> 12 us  [per_device(): pl.pallas_call(functools.partial(kernel, n_lat, n_lon, nlat), out_shape=p...]
    unnamed x1, local copies, waits for them, and re-layouts: 1.52 us -> 0.64 us
where the time goes in v2:
time: 12.8 us; the launch traced here: 12.6 us
  Pallas kernels  12 us (94%)
  local copies, waits for them, and re-layouts  0.64 us (5%)
    pallas_call x1, Pallas kernels, per_device(): pl.pallas_call(functools.partial(kernel, n_lat, n_lon, nlat), out_shape=p...  12 us
    unnamed x1, local copies, waits for them, and re-layouts  0.64 us

profile of v2, /device:TPU:1, one launch (start us, length us, event | category | flops | bytes accessed | tf_op | source)
XLA Modules:
  0.0 12.6 jit_solution(3555150386360880097)
XLA Ops:
  0.0 12.0 %shard_map.55 = f32[3,16,384]{2,1,0:T(8,128)S(1)} custom-call(f32[3,16,384]{2,1,0:T(8,128)} %bitcast.7, s32[1,16]{1,0:T(1,128)} %bitcast.8, f32[4,16]{1,0:T(4,128)} %lonw_in.1, s32[1,128]{1,0:T(1,128)} %bitcast.9, f32[4,128]{1,0:T(4,128)} %latw_in.1), custom_call_target="tpu_custom_call" | custom-call | tf_op jit(solution)/shard_map/pallas_call | solution.py:198
  12.0 0.6 %copy.8 = f32[3,1,16,384]{3,2,1,0:T(8,128)} copy(f32[3,1,16,384]{3,2,1,0:T(8,128)S(1)} %bitcast.6) | data formatting | bytes 147456

commit v3 on v2

--- a/solution.py
+++ b/solution.py
@@ -17,7 +17,7 @@
 
 def kernel(n_lat, n_lon, nlat, tr, lono_in, lonw_in, lato_in, latw_in, out,
            own, lono, lonw, lato, latw, send_r, send_l, from_l, from_r, ext,
-           own_sem, s_par, s_lon, r_lon, s_lat, r_lat):
+           own_sem, s_par, s_lon, r_lon, s_lat, r_lat, ready):
     fields, rows, width = own.shape
     tiles = width // LANES
     ilat = lax.axis_index("lat")
@@ -28,16 +28,15 @@
     has_hi = ilat < n_lat - 1
 
     barrier = pltpu.get_barrier_semaphore()
-    pl.semaphore_signal(barrier, inc=1, device_id=(ilat, right), device_id_type=MESH)
-    pl.semaphore_signal(barrier, inc=1, device_id=(ilat, left), device_id_type=MESH)
-
-    @pl.when(has_lo)
-    def _():
-        pl.semaphore_signal(barrier, inc=1, device_id=(ilat - 1, ilon), device_id_type=MESH)
-
-    @pl.when(has_hi)
-    def _():
-        pl.semaphore_signal(barrier, inc=1, device_id=(ilat + 1, ilon), device_id_type=MESH)
+    at_first = ilon == 0
+    at_last = ilon == n_lon - 1
+
+    def signal(semaphore, lat, lon):
+        pl.semaphore_signal(semaphore, inc=1, device_id=(lat, lon), device_id_type=MESH)
+
+    pl.when(at_first)(lambda: signal(barrier, ilat, left))
+    pl.when(jnp.logical_not(at_last))(lambda: signal(barrier, ilat, right))
+    pl.when(has_hi)(lambda: signal(barrier, ilat + 1, ilon))
 
     load = pltpu.make_async_copy(tr, own, own_sem)
     load.start()
@@ -49,6 +48,12 @@
     for copy in loads:
         copy.start()
 
+    greeted = has_lo.astype(jnp.int32) + jnp.logical_not(at_first).astype(jnp.int32) + at_last.astype(jnp.int32)
+    pl.when(greeted > 0)(lambda: pl.semaphore_wait(barrier, greeted))
+    pl.when(at_last)(lambda: signal(ready.at[0], ilat, right))
+    pl.when(jnp.logical_not(at_first))(lambda: signal(ready.at[1], ilat, left))
+    pl.when(has_lo)(lambda: signal(ready.at[2], ilat - 1, ilon))
+
     @pl.when(jnp.logical_not(has_lo))
     def _():
         ext[:, 0:SUB, :] = jnp.zeros((fields, SUB, width), jnp.float32)
@@ -71,8 +76,6 @@
         b = own[f, SUB:rows, LANES:2 * LANES]
         send_l[f, rows:, :] = jnp.where(upper8, pltpu.roll(b, HALF, 1), a)
 
-    pl.semaphore_wait(barrier, 2 + has_lo.astype(jnp.int32) + has_hi.astype(jnp.int32))
-
     lon_copies = []
     for f in range(fields):
         to_r = pltpu.make_async_remote_copy(
@@ -81,9 +84,33 @@
         to_l = pltpu.make_async_remote_copy(
             src_ref=send_l.at[f], dst_ref=from_r.at[f], send_sem=s_lon.at[1, f],
             recv_sem=r_lon.at[1, f], device_id=(ilat, left), device_id_type=MESH)
-        to_r.start()
-        to_l.start()
         lon_copies.append((to_r, to_l))
+
+    def start_right():
+        for to_r, _ in lon_copies:
+            to_r.start()
+
+    def start_left():
+        for _, to_l in lon_copies:
+            to_l.start()
+
+    @pl.when(at_last)
+    def _():
+        start_right()
+
+    @pl.when(jnp.logical_not(at_first))
+    def _():
+        start_left()
+
+    @pl.when(jnp.logical_not(at_last))
+    def _():
+        pl.semaphore_wait(ready.at[1], 1)
+        start_right()
+
+    @pl.when(at_first)
+    def _():
+        pl.semaphore_wait(ready.at[0], 1)
+        start_left()
 
     for copy in loads:
         copy.wait()
@@ -156,6 +183,8 @@
         for t in range(tiles):
             ext[f, SUB:SUB + rows, t * LANES:(t + 1) * LANES] = sums[t]
         up, down = lat_copies(f)
+        if f == 0:
+            pl.when(has_hi)(lambda: pl.semaphore_wait(ready.at[2], 1))
         pl.when(has_hi)(up.start)
         pl.when(has_lo)(down.start)
 
@@ -217,6 +246,7 @@
             pltpu.SemaphoreType.DMA((2, fields)),
             pltpu.SemaphoreType.DMA((2, fields)),
             pltpu.SemaphoreType.DMA((2, fields)),
+            pltpu.SemaphoreType.REGULAR((3,)),
         ],
         compiler_params=pltpu.CompilerParams(collective_id=0, has_side_effects=True),
     )(

time: 12.8 us -> 12.1 us (0.945)
  Pallas kernels: 12 us -> 11.3 us
    pallas_call x1, Pallas kernels: 12 us -> 11.3 us  [per_device(): pl.pallas_call(functools.partial(kernel, n_lat, n_lon, nlat), out_shape=p...]
where the time goes in v3:
time: 12.1 us; the launch traced here: 11.9 us
  Pallas kernels  11.3 us (93%)
  local copies, waits for them, and re-layouts  0.64 us (5%)
    pallas_call x1, Pallas kernels, per_device(): pl.pallas_call(functools.partial(kernel, n_lat, n_lon, nlat), out_shape=p...  11.3 us
    unnamed x1, local copies, waits for them, and re-layouts  0.64 us

profile of v3, /device:TPU:1, one launch (start us, length us, event | category | flops | bytes accessed | tf_op | source)
XLA Modules:
  0.0 11.9 jit_solution(5447958480397529377)
XLA Ops:
  0.0 11.3 %shard_map.55 = f32[3,16,384]{2,1,0:T(8,128)S(1)} custom-call(f32[3,16,384]{2,1,0:T(8,128)} %bitcast.7, s32[1,16]{1,0:T(1,128)} %bitcast.8, f32[4,16]{1,0:T(4,128)} %lonw_in.1, s32[1,128]{1,0:T(1,128)} %bitcast.9, f32[4,128]{1,0:T(4,128)} %latw_in.1), custom_call_target="tpu_custom_call" | custom-call | tf_op jit(solution)/shard_map/pallas_call | solution.py:227
  11.3 0.6 %copy.8 = f32[3,1,16,384]{3,2,1,0:T(8,128)} copy(f32[3,1,16,384]{3,2,1,0:T(8,128)S(1)} %bitcast.6) | data formatting | bytes 147456

commit v4 on v3

--- a/solution.py
+++ b/solution.py
@@ -38,8 +38,9 @@
     pl.when(jnp.logical_not(at_last))(lambda: signal(barrier, ilat, right))
     pl.when(has_hi)(lambda: signal(barrier, ilat + 1, ilon))
 
-    load = pltpu.make_async_copy(tr, own, own_sem)
-    load.start()
+    blocks = [pltpu.make_async_copy(tr.at[f], own.at[f], own_sem.at[f]) for f in range(fields)]
+    for copy in blocks:
+        copy.start()
     loads = [
         pltpu.make_async_copy(source, target, s_par.at[i])
         for i, (source, target) in enumerate(
@@ -64,53 +65,53 @@
 
     lane8 = lax.broadcasted_iota(jnp.int32, (SUB, LANES), 1)
     upper8 = lane8 >= HALF
-    load.wait()
-    for f in range(fields):
-        last = width - LANES
+    last = width - LANES
+
+    def start_right(f):
+        lon_copies[f][0].start()
+
+    def start_left(f):
+        lon_copies[f][1].start()
+
+    lon_copies = []
+    for f in range(fields):
+        lon_copies.append((
+            pltpu.make_async_remote_copy(
+                src_ref=send_r.at[f], dst_ref=from_l.at[f], send_sem=s_lon.at[0, f],
+                recv_sem=r_lon.at[0, f], device_id=(ilat, right), device_id_type=MESH),
+            pltpu.make_async_remote_copy(
+                src_ref=send_l.at[f], dst_ref=from_r.at[f], send_sem=s_lon.at[1, f],
+                recv_sem=r_lon.at[1, f], device_id=(ilat, left), device_id_type=MESH)))
+
+    for f in range(fields):
+        blocks[f].wait()
         send_r[f, 0:rows, :] = own[f, :, last:]
         a = own[f, 0:SUB, last - LANES:last]
         b = own[f, SUB:rows, last - LANES:last]
         send_r[f, rows:, :] = jnp.where(upper8, a, pltpu.roll(b, HALF, 1))
+        pl.when(at_last)(functools.partial(start_right, f))
         send_l[f, 0:rows, :] = own[f, :, 0:LANES]
         a = own[f, 0:SUB, LANES:2 * LANES]
         b = own[f, SUB:rows, LANES:2 * LANES]
         send_l[f, rows:, :] = jnp.where(upper8, pltpu.roll(b, HALF, 1), a)
-
-    lon_copies = []
-    for f in range(fields):
-        to_r = pltpu.make_async_remote_copy(
-            src_ref=send_r.at[f], dst_ref=from_l.at[f], send_sem=s_lon.at[0, f],
-            recv_sem=r_lon.at[0, f], device_id=(ilat, right), device_id_type=MESH)
-        to_l = pltpu.make_async_remote_copy(
-            src_ref=send_l.at[f], dst_ref=from_r.at[f], send_sem=s_lon.at[1, f],
-            recv_sem=r_lon.at[1, f], device_id=(ilat, left), device_id_type=MESH)
-        lon_copies.append((to_r, to_l))
-
-    def start_right():
-        for to_r, _ in lon_copies:
-            to_r.start()
-
-    def start_left():
-        for _, to_l in lon_copies:
-            to_l.start()
+        pl.when(jnp.logical_not(at_first | at_last))(functools.partial(start_left, f))
 
     @pl.when(at_last)
     def _():
-        start_right()
-
-    @pl.when(jnp.logical_not(at_first))
-    def _():
-        start_left()
+        for f in range(fields):
+            start_left(f)
 
     @pl.when(jnp.logical_not(at_last))
     def _():
         pl.semaphore_wait(ready.at[1], 1)
-        start_right()
+        for f in range(fields):
+            start_right(f)
 
     @pl.when(at_first)
     def _():
         pl.semaphore_wait(ready.at[0], 1)
-        start_left()
+        for f in range(fields):
+            start_left(f)
 
     for copy in loads:
         copy.wait()
@@ -240,7 +241,7 @@
             pltpu.VMEM((fields, rows + SUB, LANES), jnp.float32),
             pltpu.VMEM((fields, rows + SUB, LANES), jnp.float32),
             pltpu.VMEM((fields, rows + 2 * SUB, width), jnp.float32),
-            pltpu.SemaphoreType.DMA,
+            pltpu.SemaphoreType.DMA((fields,)),
             pltpu.SemaphoreType.DMA((4,)),
             pltpu.SemaphoreType.DMA((2, fields)),
             pltpu.SemaphoreType.DMA((2, fields)),

time: 12.1 us -> 11.9 us (0.983)
  Pallas kernels: 11.3 us -> 11.1 us
    pallas_call x1, Pallas kernels: 11.3 us -> 11.1 us  [per_device(): pl.pallas_call(functools.partial(kernel, n_lat, n_lon, nlat), out_shape=p...]
where the time goes in v4:
time: 11.9 us; the launch traced here: 11.8 us
  Pallas kernels  11.1 us (93%)
  local copies, waits for them, and re-layouts  0.64 us (5%)
    pallas_call x1, Pallas kernels, per_device(): pl.pallas_call(functools.partial(kernel, n_lat, n_lon, nlat), out_shape=p...  11.1 us
    unnamed x1, local copies, waits for them, and re-layouts  0.64 us

profile of v4, /device:TPU:1, one launch (start us, length us, event | category | flops | bytes accessed | tf_op | source)
XLA Modules:
  0.0 11.8 jit_solution(11424783926150657131)
XLA Ops:
  0.0 11.1 %shard_map.55 = f32[3,16,384]{2,1,0:T(8,128)S(1)} custom-call(f32[3,16,384]{2,1,0:T(8,128)} %bitcast.7, s32[1,16]{1,0:T(1,128)} %bitcast.8, f32[4,16]{1,0:T(4,128)} %lonw_in.1, s32[1,128]{1,0:T(1,128)} %bitcast.9, f32[4,128]{1,0:T(4,128)} %latw_in.1), custom_call_target="tpu_custom_call" | custom-call | tf_op jit(solution)/shard_map/pallas_call | solution.py:228
  11.1 0.6 %copy.8 = f32[3,1,16,384]{3,2,1,0:T(8,128)} copy(f32[3,1,16,384]{3,2,1,0:T(8,128)S(1)} %bitcast.6) | data formatting | bytes 147456

commit v5 on v4

--- a/solution.py
+++ b/solution.py
@@ -27,6 +27,10 @@
     has_lo = ilat > 0
     has_hi = ilat < n_lat - 1
 
+    blocks = [pltpu.make_async_copy(tr.at[f], own.at[f], own_sem.at[f]) for f in range(fields)]
+    for copy in blocks:
+        copy.start()
+
     barrier = pltpu.get_barrier_semaphore()
     at_first = ilon == 0
     at_last = ilon == n_lon - 1
@@ -38,9 +42,6 @@
     pl.when(jnp.logical_not(at_last))(lambda: signal(barrier, ilat, right))
     pl.when(has_hi)(lambda: signal(barrier, ilat + 1, ilon))
 
-    blocks = [pltpu.make_async_copy(tr.at[f], own.at[f], own_sem.at[f]) for f in range(fields)]
-    for copy in blocks:
-        copy.start()
     loads = [
         pltpu.make_async_copy(source, target, s_par.at[i])
         for i, (source, target) in enumerate(
@@ -162,8 +163,8 @@
     partial = []
     for f in range(fields):
         to_r, to_l = lon_copies[f]
+        to_l.wait_recv()
         to_r.wait_recv()
-        to_l.wait_recv()
         tail_l = from_l[f, rows:, :]
         tail_r = from_r[f, rows:, :]
         x = [jnp.concatenate([tail_l, pltpu.roll(tail_l, HALF, 1)], axis=0), from_l[f, 0:rows, :]]
@@ -184,10 +185,10 @@
         for t in range(tiles):
             ext[f, SUB:SUB + rows, t * LANES:(t + 1) * LANES] = sums[t]
         up, down = lat_copies(f)
+        pl.when(has_lo)(down.start)
         if f == 0:
             pl.when(has_hi)(lambda: pl.semaphore_wait(ready.at[2], 1))
         pl.when(has_hi)(up.start)
-        pl.when(has_lo)(down.start)
 
     for f in range(fields):
         low = jnp.zeros((SUB, width), jnp.float32)

time: 11.9 us -> 11.9 us (level)
  no operation moved by 1% of the time
where the time goes in v5:
time: 11.9 us; the launch traced here: 11.7 us
  Pallas kernels  11.1 us (93%)
  local copies, waits for them, and re-layouts  0.64 us (5%)
    pallas_call x1, Pallas kernels, per_device(): pl.pallas_call(functools.partial(kernel, n_lat, n_lon, nlat), out_shape=p...  11.1 us
    unnamed x1, local copies, waits for them, and re-layouts  0.64 us

profile of v5, /device:TPU:1, one launch (start us, length us, event | category | flops | bytes accessed | tf_op | source)
XLA Modules:
  0.0 11.7 jit_solution(14276554181228984629)
XLA Ops:
  0.0 11.1 %shard_map.55 = f32[3,16,384]{2,1,0:T(8,128)S(1)} custom-call(f32[3,16,384]{2,1,0:T(8,128)} %bitcast.7, s32[1,16]{1,0:T(1,128)} %bitcast.8, f32[4,16]{1,0:T(4,128)} %lonw_in.1, s32[1,128]{1,0:T(1,128)} %bitcast.9, f32[4,128]{1,0:T(4,128)} %latw_in.1), custom_call_target="tpu_custom_call" | custom-call | tf_op jit(solution)/shard_map/pallas_call | solution.py:229
  11.1 0.6 %copy.8 = f32[3,1,16,384]{3,2,1,0:T(8,128)} copy(f32[3,1,16,384]{3,2,1,0:T(8,128)S(1)} %bitcast.6) | data formatting | bytes 147456
